TPU v7x, 32 devices: a whole 2x2x4 slice. The times are simulated.
32 devices in a mesh: dp: 2 (over core), region: 16 (over z, y, x).
Axes of the slice: x: 2, y: 2, z: 4, core: 2. Of those that a mesh axis runs over, the one named last changes fastest.
Arguments:
- cell_counts: int32 [16384], P('dp'), may hold values from 61 to 6144, as said below
- cell_seeds: int32 [16384], P('dp'), may hold values from 0 to 12287
- batch_ids: int32 [16384], P('dp'), may hold values from 0 to 7
- noise_draw: float32 [16384, 10], P('dp'), may hold values from -4 to 4
- cell_factor: float32 [16384], P('dp'), may hold values from 0.3 to 0.95
- enc_weight: float32 [12288, 128], P('region', 'dp'), may hold values from -0.0546875 to 0.0546875
- enc_first: float32 [12288, 128], P('region', 'dp'), may hold values from -1.1444092e-05 to 1.1444092e-05
- enc_second: float32 [12288, 128], P('region', 'dp'), may hold values from 3.4924596e-12 to 1.3969838e-11
- dec_weight: float32 [128, 12288], P('dp', 'region'), may hold values from -0.5 to 0.5
- dec_first: float32 [128, 12288], P('dp', 'region'), may hold values from -7.1525574e-07 to 7.1525574e-07
- dec_second: float32 [128, 12288], P('dp', 'region'), may hold values from 1.6168795e-14 to 6.467518e-14
- region_vecs: float32 [2, 12288], P('dp', 'region')
- vec_first: float32 [2, 12288], P('dp', 'region'), may hold values from -1.335144e-05 to 1.335144e-05
- vec_second: float32 [2, 12288], P('dp', 'region'), may hold values from 4.6566128e-12 to 1.8626451e-11
- trunk_rows: float32 [290, 128], replicated
- trunk_first: float32 [290, 128], replicated, may hold values from -1.5258789e-05 to 1.5258789e-05
- trunk_second: float32 [290, 128], replicated, may hold values from 6.2088173e-12 to 2.483527e-11
- head_rows: float32 [129, 20], replicated
- head_first: float32 [129, 20], replicated, may hold values from -1.5258789e-05 to 1.5258789e-05
- head_second: float32 [129, 20], replicated, may hold values from 6.2088173e-12 to 2.483527e-11
Outputs:
- loss: float32 [2], replicated
- enc_new: float32 [12288, 128], P('region', 'dp')
- enc_first_new: float32 [12288, 128], P('region', 'dp')
- enc_second_new: float32 [12288, 128], P('region', 'dp')
- enc_copy: bfloat16 [12288, 128], P('region', 'dp')
- dec_new: float32 [128, 12288], P('dp', 'region')
- dec_first_new: float32 [128, 12288], P('dp', 'region')
- dec_second_new: float32 [128, 12288], P('dp', 'region')
- dec_copy: bfloat16 [128, 12288], P('dp', 'region')
- vecs_new: float32 [2, 12288], P('dp', 'region')
- vec_first_new: float32 [2, 12288], P('dp', 'region')
- vec_second_new: float32 [2, 12288], P('dp', 'region')
- trunk_new: float32 [290, 128], replicated
- trunk_first_new: float32 [290, 128], replicated
- trunk_second_new: float32 [290, 128], replicated
- head_new: float32 [129, 20], replicated
- head_first_new: float32 [129, 20], replicated
- head_second_new: float32 [129, 20], replicated
- norms: float32 [2, 10], replicated
Inputs may be any that keep to these rules, and one draw needn't show every extreme that they name: Each cell opens exactly cell_counts regions, given by the rule of the first step; some cell holds the smallest and some the largest count.
All inputs are finite; a program needn't handle non-finite values.
Results may differ from a plain program's by a relative error of at most 0.002.
The roundings to bfloat16 on the way count: a program that leaves them out, or rounds other values in their place, can miss the bound.
Values may be sent and summed in bfloat16 or wider, within the bound.
No kernel may reach another device: no remote copies, remote signals or barrier semaphores. Data moves between devices by JAX's collectives and lax.ppermute only.
A program may use at most 128 MiB of HBM per device.

v0:
```python
import jax
import jax.numpy as jnp
from jax import lax
from jax.sharding import PartitionSpec as P

BATCHES = 8
highest = lax.Precision.HIGHEST
norm_eps = 1e-05
leak_slope = 0.01
decay_rate = 0.5
weight_decay = 0.01
learn_rate = 0.5
lamb_eps = 1e-12


def matmul(left, right):
    return jnp.dot(left, right, precision=highest, preferred_element_type=jnp.float32)


def layer_norm(values, gain_row, shift_row):
    centre = values - jnp.mean(values, axis=-1, keepdims=True)
    spread = jnp.mean(centre * centre, axis=-1, keepdims=True)
    return centre * lax.rsqrt(spread + norm_eps) * gain_row + shift_row


def leaky_relu(values):
    return jnp.where(values >= 0, values, leak_slope * values)


def region_masks(counts, seed_rows, first_region, width, total):
    regions = first_region + jnp.arange(width, dtype=jnp.int32)
    stride = 6 * (seed_rows % (total // 6)) + 1
    upper = stride[:, None] * (regions[None, :] // 256) % total
    hashed = (upper * 256 + stride[:, None] * (regions[None, :] % 256) + seed_rows[:, None]) % total
    return hashed < counts[:, None]


def trunk_forward(pre_in, trunk_part, head_part, noise_rows, onehot):
    hidden = trunk_part.shape[1]
    latent = head_part.shape[1] // 2
    batches = onehot.shape[1]
    enc_two = trunk_part[batches : batches + hidden]
    dec_one = trunk_part[batches + hidden : 2 * batches + hidden + latent]
    dec_two = trunk_part[2 * batches + hidden + latent : 2 * batches + 2 * hidden + latent]
    base_row = 2 * batches + 2 * hidden + latent
    gain_rows = trunk_part[base_row : base_row + 4]
    shift_rows = trunk_part[base_row + 4 : base_row + 8]
    first = leaky_relu(layer_norm(pre_in, gain_rows[0], shift_rows[0]))
    second = leaky_relu(layer_norm(matmul(first, enc_two), gain_rows[1], shift_rows[1]))
    moments = matmul(second, head_part[:hidden]) + head_part[hidden]
    centre_lat = moments[:, :latent]
    log_var = moments[:, latent:]
    sample = centre_lat + jnp.exp(0.5 * log_var) * noise_rows
    third_in = matmul(sample, dec_one[:latent]) + matmul(onehot, dec_one[latent:])
    third = leaky_relu(layer_norm(third_in, gain_rows[2], shift_rows[2]))
    fourth = leaky_relu(layer_norm(matmul(third, dec_two), gain_rows[3], shift_rows[3]))
    diverge = 0.5 * jnp.sum(jnp.exp(log_var) + centre_lat * centre_lat - 1.0 - log_var)
    return (fourth, diverge)


def lamb_moments(weight, grad, first, second):
    first_new = decay_rate * first + (1.0 - decay_rate) * grad
    second_new = decay_rate * second + (1.0 - decay_rate) * grad * grad
    update = first_new / (jnp.sqrt(second_new) + lamb_eps) + weight_decay * weight
    return (first_new, second_new, update)


def square_norm(values):
    return jnp.sqrt(jnp.sum(values * values))


def lamb_groups(weight, update, row_edges):
    pieces = []
    weight_list = []
    update_list = []
    for group_index in range(len(row_edges) - 1):
        start_row = row_edges[group_index]
        end_row = row_edges[group_index + 1]
        weight_part = weight[start_row:end_row]
        update_part = update[start_row:end_row]
        weight_norm = square_norm(weight_part)
        update_norm = square_norm(update_part)
        weight_list.append(weight_norm)
        update_list.append(update_norm)
        pieces.append(weight_part - learn_rate * (weight_norm / update_norm) * update_part)
    return (jnp.concatenate(pieces, axis=0), jnp.stack(weight_list), jnp.stack(update_list))


def weight_squares(enc_weight, dec_weight, region_vecs, slot_rows):
    pair = jnp.stack([jnp.sum(enc_weight * enc_weight), jnp.sum(dec_weight * dec_weight)])
    return jnp.concatenate([pair, slot_rows * jnp.sum(region_vecs * region_vecs)])


def on_device(
    cell_counts,
    cell_seeds,
    batch_ids,
    noise_draw,
    cell_factor,
    enc_weight,
    enc_first,
    enc_second,
    dec_weight,
    dec_first,
    dec_second,
    region_vecs,
    vec_first,
    vec_second,
    trunk_rows,
    trunk_first,
    trunk_second,
    head_rows,
    head_first,
    head_second,
):
    cells_here = cell_counts.shape[0]
    regions_here = enc_weight.shape[0]
    hidden = trunk_rows.shape[1]
    latent = head_rows.shape[1] // 2
    region_count = lax.axis_size("region")
    total_regions = regions_here * region_count
    all_cells = cells_here * lax.axis_size("dp")
    loss_scale = 1.0 / (all_cells * total_regions)
    first_region = lax.axis_index("region") * regions_here
    row_index = lax.axis_index("dp")
    slot_rows = (jnp.arange(2, dtype=jnp.int32) == row_index).astype(jnp.float32)
    block_rows = min(1024, cells_here)
    blocks = cells_here // block_rows
    enc_low, dec_low, vec_low = (
        lax.all_gather(enc_weight.astype(jnp.bfloat16), "dp", axis=1, tiled=True),
        lax.all_gather(dec_weight.astype(jnp.bfloat16), "dp", axis=0, tiled=True),
        lax.all_gather(region_vecs.astype(jnp.bfloat16), "dp", axis=0, tiled=True),
    )
    counts_blocks = cell_counts.reshape(blocks, block_rows)
    seed_blocks = cell_seeds.reshape(blocks, block_rows)

    def encode_block(carried, inputs):
        mask_rows = region_masks(
            inputs[0], inputs[1], first_region, regions_here, total_regions
        ).astype(jnp.bfloat16)
        return (carried, jnp.dot(mask_rows, enc_low, preferred_element_type=jnp.float32))

    _, partial_pre = lax.scan(
        encode_block, jnp.zeros((), jnp.float32), (counts_blocks, seed_blocks)
    )
    partial_pre = partial_pre.reshape(cells_here, hidden)
    onehot = (batch_ids[:, None] == jnp.arange(BATCHES, dtype=jnp.int32)[None, :]).astype(
        jnp.float32
    )
    onehot_low = onehot.astype(jnp.bfloat16)
    enc_total = lax.psum(partial_pre, "region")
    pre_one = enc_total + matmul(onehot, trunk_rows[:BATCHES])
    (decoded, diverge), pull_back = jax.vjp(
        lambda pre_in, weights, head_part: trunk_forward(
            pre_in, weights, head_part, noise_draw, onehot
        ),
        pre_one,
        trunk_rows,
        head_rows,
    )
    decoded_low = decoded.astype(jnp.bfloat16)
    decoded_blocks = decoded_low.reshape(blocks, block_rows, hidden)
    factor_blocks = cell_factor.reshape(blocks, block_rows)
    region_bias = vec_low[0].astype(jnp.float32)
    region_logit = vec_low[1].astype(jnp.float32)
    log_region = jax.nn.log_sigmoid(region_logit)
    keep_region = jax.nn.sigmoid(-region_logit)

    def decode_block(carried, inputs):
        grad_dec, grad_bias, grad_logit, recon_sum = carried
        counts, seed_rows, hidden_low, factors = inputs
        mask_rows = region_masks(
            counts, seed_rows, first_region, regions_here, total_regions
        ).astype(jnp.float32)
        logits = jnp.dot(hidden_low, dec_low, preferred_element_type=jnp.float32) + region_bias
        log_prob = jax.nn.log_sigmoid(logits) + jnp.log(factors)[:, None] + log_region[None, :]
        probability = jnp.exp(log_prob)
        recon_sum = recon_sum - jnp.sum(
            mask_rows * log_prob + (1.0 - mask_rows) * jnp.log1p(-probability)
        )
        signal = (mask_rows - (1.0 - mask_rows) * probability / (1.0 - probability)) * loss_scale
        grad_logits = (-jax.nn.sigmoid(-logits) * signal).astype(jnp.bfloat16)
        grad_dec = grad_dec + lax.dot_general(
            hidden_low, grad_logits, (((0,), (0,)), ((), ())), preferred_element_type=jnp.float32
        )
        grad_bias = grad_bias + jnp.sum(grad_logits, axis=0, dtype=jnp.float32)
        grad_logit = grad_logit - keep_region * jnp.sum(signal, axis=0)
        back_part = lax.dot_general(
            grad_logits, dec_low, (((1,), (1,)), ((), ())), preferred_element_type=jnp.float32
        )
        return ((grad_dec, grad_bias, grad_logit, recon_sum), back_part)

    initial = (
        jnp.zeros((hidden, regions_here), jnp.float32),
        jnp.zeros((regions_here,), jnp.float32),
        jnp.zeros((regions_here,), jnp.float32),
        jnp.zeros((), jnp.float32),
    )
    (grad_dec, grad_bias, grad_logit, recon_sum), back_parts = lax.scan(
        decode_block, initial, (counts_blocks, seed_blocks, decoded_blocks, factor_blocks)
    )
    back_hidden = back_parts.reshape(cells_here, hidden)
    hidden_grad, recon_region = lax.psum((back_hidden, recon_sum), "region")
    grad_pre, grad_trunk, grad_head = pull_back((hidden_grad, jnp.float32(loss_scale)))
    pre_low = grad_pre.astype(jnp.bfloat16)
    batch_grad = lax.dot_general(
        onehot_low, pre_low, (((0,), (0,)), ((), ())), preferred_element_type=jnp.float32
    )
    grad_trunk = grad_trunk.at[:BATCHES].add(batch_grad)
    grad_trunk, grad_head, recon_all, diverge_all = lax.psum(
        (grad_trunk, grad_head, recon_region, diverge), "dp"
    )
    pre_blocks = pre_low.reshape(blocks, block_rows, hidden)

    def encode_back(carried, inputs):
        mask_rows = region_masks(
            inputs[0], inputs[1], first_region, regions_here, total_regions
        ).astype(jnp.bfloat16)
        return (
            carried
            + lax.dot_general(
                mask_rows, inputs[2], (((0,), (0,)), ((), ())), preferred_element_type=jnp.float32
            ),
            None,
        )

    grad_enc, _ = lax.scan(
        encode_back,
        jnp.zeros((regions_here, hidden), jnp.float32),
        (counts_blocks, seed_blocks, pre_blocks),
    )
    grad_vecs = jnp.stack([grad_bias, grad_logit])
    grad_enc, grad_dec, grad_vecs = (
        lax.psum_scatter(grad_enc, "dp", scatter_dimension=1, tiled=True),
        lax.psum_scatter(grad_dec, "dp", scatter_dimension=0, tiled=True),
        lax.psum_scatter(grad_vecs, "dp", scatter_dimension=0, tiled=True),
    )
    enc_first_new, enc_second_new, enc_update = lamb_moments(
        enc_weight, grad_enc, enc_first, enc_second
    )
    dec_first_new, dec_second_new, dec_update = lamb_moments(
        dec_weight, grad_dec, dec_first, dec_second
    )
    vec_first_new, vec_second_new, vec_update = lamb_moments(
        region_vecs, grad_vecs, vec_first, vec_second
    )
    update_local = weight_squares(enc_update, dec_update, vec_update, slot_rows)
    weight_sums, update_sums = lax.psum(
        (weight_squares(enc_weight, dec_weight, region_vecs, slot_rows), update_local),
        ("dp", "region"),
    )
    region_wn = jnp.sqrt(weight_sums)
    region_un = jnp.sqrt(update_sums)
    enc_new = enc_weight - learn_rate * (region_wn[0] / region_un[0]) * enc_update
    dec_new = dec_weight - learn_rate * (region_wn[1] / region_un[1]) * dec_update
    vec_ratio = jnp.where(row_index == 0, region_wn[2] / region_un[2], region_wn[3] / region_un[3])
    vecs_new = region_vecs - learn_rate * vec_ratio * vec_update
    trunk_first_new, trunk_second_new, trunk_update = lamb_moments(
        trunk_rows, grad_trunk, trunk_first, trunk_second
    )
    head_first_new, head_second_new, head_update = lamb_moments(
        head_rows, grad_head, head_first, head_second
    )
    row_edges = [
        0,
        BATCHES,
        BATCHES + hidden,
        2 * BATCHES + hidden + latent,
        2 * BATCHES + 2 * hidden + latent,
        2 * BATCHES + 2 * hidden + latent + 8,
    ]
    trunk_new, trunk_wn, trunk_un = lamb_groups(trunk_rows, trunk_update, row_edges)
    head_new, head_wn, head_un = lamb_groups(head_rows, head_update, [0, hidden + 1])
    norms = jnp.stack(
        [
            jnp.concatenate([region_wn, trunk_wn, head_wn]),
            jnp.concatenate([region_un, trunk_un, head_un]),
        ]
    )
    loss = jnp.stack([recon_all * loss_scale, diverge_all / all_cells])
    return (
        loss,
        enc_new,
        enc_first_new,
        enc_second_new,
        enc_new.astype(jnp.bfloat16),
        dec_new,
        dec_first_new,
        dec_second_new,
        dec_new.astype(jnp.bfloat16),
        vecs_new,
        vec_first_new,
        vec_second_new,
        trunk_new,
        trunk_first_new,
        trunk_second_new,
        head_new,
        head_first_new,
        head_second_new,
        norms,
    )


def solution(mesh):
    return jax.shard_map(
        on_device,
        mesh=mesh,
        in_specs=(
            P("dp"),
            P("dp"),
            P("dp"),
            P("dp", None),
            P("dp"),
            P("region", "dp"),
            P("region", "dp"),
            P("region", "dp"),
            P("dp", "region"),
            P("dp", "region"),
            P("dp", "region"),
            P("dp", "region"),
            P("dp", "region"),
            P("dp", "region"),
            P(),
            P(),
            P(),
            P(),
            P(),
            P(),
        ),
        out_specs=(
            P(),
            P("region", "dp"),
            P("region", "dp"),
            P("region", "dp"),
            P("region", "dp"),
            P("dp", "region"),
            P("dp", "region"),
            P("dp", "region"),
            P("dp", "region"),
            P("dp", "region"),
            P("dp", "region"),
            P("dp", "region"),
            P(),
            P(),
            P(),
            P(),
            P(),
            P(),
            P(),
        ),
        check_vma=False,
    )
```

profile of v0, /device:TPU:0, one launch (start us, length us, event | category | flops | bytes accessed | tf_op | source)
XLA Modules:
  0.0 877.8 jit_solution(4330750522462627467)
XLA Ops:
  13.2 2.3 broadcast.824.clone
  15.5 51.1 %while.50 = (s32[]{:T(128)}, f32[8,1024,128]{2,1,0:T(8,128)}, s32[8,1024]{1,0:T(8,128)}, s32[]{:T(128)}, s32[8,1024]{1,0:T(8,128)}, /*index=5*/bf16[768,128]{1,0:T(8,128)(2,1)S(1)}, s32[]{:T(128)}) while((s32[]{:T(128)}, f32[8,1024,128]{2,1,0:T(8,128)}, s32[8,1024]{1,0:T(8,128)}, s32[]{:T(128)}, s32[8,1024]{1,0:T(8,128)}, ...), condition=%wide.region_1.2_spmd, body=%wide.region_0.1_spmd.sunk | while | flops 215511040 | bytes 770645 | solution.py:143
  16.3 5.6 fusion.253
  22.7 5.6 fusion.253
  29.1 5.6 fusion.253
  35.5 5.6 fusion.253
  41.8 5.6 fusion.253
  48.2 5.6 fusion.253
  54.6 5.6 fusion.253
  61.0 5.6 fusion.253
  72.8 164.7 %all-reduce.26.cloned.1.call-done = f32[8192,128]{1,0:T(8,128)} async-done(((f32[8192,128]{1,0:T(8,128)}), f32[8192,128]{1,0:T(8,128)}) %all-reduce.26.cloned.1.call-update) | async-done | bytes 4194320 | tf_op jit(solution)/shard_map/psum | solution.py:151
  237.6 6.2 fusion.224
  243.8 2.4 multiply_reduce_fusion.11
  246.2 8.2 fusion.225
  254.4 5.6 copy.58
  260.0 4.6 multiply_reduce_fusion.10
  264.8 5.1 convolution_add_fusion.3
  269.9 6.7 fusion.188
  276.6 4.6 fusion.226
  281.2 2.4 multiply_reduce_fusion.9
  283.7 4.9 fusion.227
  288.6 2.4 multiply_reduce_fusion.8
  291.6 5.3 fusion.102
  299.3 146.1 %while.51 = (s32[]{:T(128)}, f32[128,768]{1,0:T(8,128)S(1)}, f32[768]{0:T(1024)S(1)}, f32[768]{0:T(1024)}, f32[]{:T(128)}, /*index=5*/f32[8,1024,128]{2,1,0:T(8,...) while((s32[]{:T(128)}, f32[128,768]{1,0:T(8,128)S(1)}, ...), condition=%wide.region_15.16_spmd.clone, body=%wide.region_11.15_spmd.clone.sunk | while | flops 643528960 | bytes 19630788 | solution.py:199
  301.1 10.9 %fusion.260 = (f32[768]{0:T(1024)}, f32[1024,768]{1,0:T(8,128)S(1)}, f32[]{:T(128)}, f32[1024,768]{1,0:T(8,128)S(1)}) fusion(f32[768]{0:T(1024)} %get-tuple-element.1021, f32[1024]{0:T(1024)S(1)} %bitcast.133, f32[768]{0:T(1024)S(1)} %get-tuple-element.1016, s32[1024]{0:T(1024)S(1)} %bitcast.134, s32[1024]{0:T(1024)S(1)} %bitcast.128, ...), kind=kOutput, calls=%fused_computation.378.clone.1 | convolution fusion | flops 234355968 | bytes 6783492 | tf_op jit(solution)/shard_map/while/body/eval_jaxpr/dot_general | solution.py:175
  319.3 10.9 %fusion.260 = (f32[768]{0:T(1024)}, f32[1024,768]{1,0:T(8,128)S(1)}, f32[]{:T(128)}, f32[1024,768]{1,0:T(8,128)S(1)}) fusion(f32[768]{0:T(1024)} %get-tuple-element.1021, f32[1024]{0:T(1024)S(1)} %bitcast.133, f32[768]{0:T(1024)S(1)} %get-tuple-element.1016, s32[1024]{0:T(1024)S(1)} %bitcast.134, s32[1024]{0:T(1024)S(1)} %bitcast.128, ...), kind=kOutput, calls=%fused_computation.378.clone.1 | convolution fusion | flops 234355968 | bytes 6783492 | tf_op jit(solution)/shard_map/while/body/eval_jaxpr/dot_general | solution.py:175
  337.5 10.9 %fusion.260 = (f32[768]{0:T(1024)}, f32[1024,768]{1,0:T(8,128)S(1)}, f32[]{:T(128)}, f32[1024,768]{1,0:T(8,128)S(1)}) fusion(f32[768]{0:T(1024)} %get-tuple-element.1021, f32[1024]{0:T(1024)S(1)} %bitcast.133, f32[768]{0:T(1024)S(1)} %get-tuple-element.1016, s32[1024]{0:T(1024)S(1)} %bitcast.134, s32[1024]{0:T(1024)S(1)} %bitcast.128, ...), kind=kOutput, calls=%fused_computation.378.clone.1 | convolution fusion | flops 234355968 | bytes 6783492 | tf_op jit(solution)/shard_map/while/body/eval_jaxpr/dot_general | solution.py:175
  355.8 10.9 %fusion.260 = (f32[768]{0:T(1024)}, f32[1024,768]{1,0:T(8,128)S(1)}, f32[]{:T(128)}, f32[1024,768]{1,0:T(8,128)S(1)}) fusion(f32[768]{0:T(1024)} %get-tuple-element.1021, f32[1024]{0:T(1024)S(1)} %bitcast.133, f32[768]{0:T(1024)S(1)} %get-tuple-element.1016, s32[1024]{0:T(1024)S(1)} %bitcast.134, s32[1024]{0:T(1024)S(1)} %bitcast.128, ...), kind=kOutput, calls=%fused_computation.378.clone.1 | convolution fusion | flops 234355968 | bytes 6783492 | tf_op jit(solution)/shard_map/while/body/eval_jaxpr/dot_general | solution.py:175
  374.0 10.9 %fusion.260 = (f32[768]{0:T(1024)}, f32[1024,768]{1,0:T(8,128)S(1)}, f32[]{:T(128)}, f32[1024,768]{1,0:T(8,128)S(1)}) fusion(f32[768]{0:T(1024)} %get-tuple-element.1021, f32[1024]{0:T(1024)S(1)} %bitcast.133, f32[768]{0:T(1024)S(1)} %get-tuple-element.1016, s32[1024]{0:T(1024)S(1)} %bitcast.134, s32[1024]{0:T(1024)S(1)} %bitcast.128, ...), kind=kOutput, calls=%fused_computation.378.clone.1 | convolution fusion | flops 234355968 | bytes 6783492 | tf_op jit(solution)/shard_map/while/body/eval_jaxpr/dot_general | solution.py:175
  392.3 10.9 %fusion.260 = (f32[768]{0:T(1024)}, f32[1024,768]{1,0:T(8,128)S(1)}, f32[]{:T(128)}, f32[1024,768]{1,0:T(8,128)S(1)}) fusion(f32[768]{0:T(1024)} %get-tuple-element.1021, f32[1024]{0:T(1024)S(1)} %bitcast.133, f32[768]{0:T(1024)S(1)} %get-tuple-element.1016, s32[1024]{0:T(1024)S(1)} %bitcast.134, s32[1024]{0:T(1024)S(1)} %bitcast.128, ...), kind=kOutput, calls=%fused_computation.378.clone.1 | convolution fusion | flops 234355968 | bytes 6783492 | tf_op jit(solution)/shard_map/while/body/eval_jaxpr/dot_general | solution.py:175
  410.5 10.9 %fusion.260 = (f32[768]{0:T(1024)}, f32[1024,768]{1,0:T(8,128)S(1)}, f32[]{:T(128)}, f32[1024,768]{1,0:T(8,128)S(1)}) fusion(f32[768]{0:T(1024)} %get-tuple-element.1021, f32[1024]{0:T(1024)S(1)} %bitcast.133, f32[768]{0:T(1024)S(1)} %get-tuple-element.1016, s32[1024]{0:T(1024)S(1)} %bitcast.134, s32[1024]{0:T(1024)S(1)} %bitcast.128, ...), kind=kOutput, calls=%fused_computation.378.clone.1 | convolution fusion | flops 234355968 | bytes 6783492 | tf_op jit(solution)/shard_map/while/body/eval_jaxpr/dot_general | solution.py:175
  428.7 10.9 %fusion.260 = (f32[768]{0:T(1024)}, f32[1024,768]{1,0:T(8,128)S(1)}, f32[]{:T(128)}, f32[1024,768]{1,0:T(8,128)S(1)}) fusion(f32[768]{0:T(1024)} %get-tuple-element.1021, f32[1024]{0:T(1024)S(1)} %bitcast.133, f32[768]{0:T(1024)S(1)} %get-tuple-element.1016, s32[1024]{0:T(1024)S(1)} %bitcast.134, s32[1024]{0:T(1024)S(1)} %bitcast.128, ...), kind=kOutput, calls=%fused_computation.378.clone.1 | convolution fusion | flops 234355968 | bytes 6783492 | tf_op jit(solution)/shard_map/while/body/eval_jaxpr/dot_general | solution.py:175
  452.9 43.1 %psum.64 = f32[]{:T(128)} all-reduce(f32[]{:T(128)} %get-tuple-element.495), channel_id=1, replica_groups=mesh['dp'=2,'region'=16] {'region'}, use_global_device_ids=true, to_apply=%region_16.17 | all-reduce | flops 1 | bytes 8 | tf_op jit(solution)/shard_map/psum | solution.py:203
  496.1 2.4 multiply_reduce_fusion.12
  498.5 130.4 %all-reduce.28.cloned.1.call-done = f32[8192,128]{1,0:T(8,128)} async-done(((f32[8192,128]{1,0:T(8,128)}), f32[8192,128]{1,0:T(8,128)}) %all-reduce.28.cloned.1.call-update) | async-done | bytes 4194320 | tf_op jit(solution)/shard_map/psum | solution.py:203
  628.9 7.6 fusion.208
  636.6 5.1 fusion.221
  641.8 6.4 multiply_reduce_fusion.2
  648.3 5.3 fusion.220
  653.6 4.5 multiply_add_fusion.9
  658.4 4.4 fusion.122
  662.8 11.2 %multiply_reduce_fusion.1 = (f32[128]{0:T(128)}, f32[8192]{0:T(1024)S(1)}, f32[128]{0:T(128)}, f32[8192,128]{1,0:T(8,128)S(1)}) fusion(f32[8192,128]{1,0:T(8,128)S(1)} %copy-done.3, f32[8192]{0:T(1024)S(1)} %copy-done.50, f32[8192]{0:T(1024)S(1)} %copy-done.29, f32[128]{0:T(128)S(1)} %copy-done.67, f32[129,20]{0,1:T(8,128)S(1)} %copy-done.44, ...), kind=kOutput, calls=%fused_computation.162 | convolution fusion | flops 267542272 | bytes 9549824 | tf_op jit(solution)/shard_map/transpose(jvp())/dot_general | solution.py:17
  673.9 11.3 %fusion.109 = f32[128,128]{1,0:T(8,128)} fusion(f32[8192,128]{1,0:T(8,128)S(1)} %get-tuple-element.698, f32[8192,128]{1,0:T(8,128)S(1)} %copy-done.7, f32[8192]{0:T(1024)S(1)} %negate_multiply_fusion.3, f32[128]{0:T(128)S(1)} %copy-done.75, f32[128]{0:T(128)S(1)} %copy-done.69, f32[8192]{0:T(1024)S(1)} %copy-done.52, f32[8192]{0:T(1024)S(1)} %copy-done.31), kind=kOutput, calls=%fused_computation.186 | convolution fusion | flops 1619001344 | bytes 8553472 | tf_op jit(solution)/shard_map/transpose(jvp())/dot_general | solution.py:17
  685.2 2.5 fusion.117
  687.7 2.7 fusion.115
  690.5 5.1 fusion.218
  695.7 8.0 multiply_reduce_fusion
  703.7 10.9 %fusion.103 = f32[128,128]{1,0:T(8,128)} fusion(f32[8192,128]{1,0:T(8,128)S(1)} %get-tuple-element.692, f32[8192,128]{1,0:T(8,128)S(1)} %copy-done.5, f32[8192]{0:T(1024)S(1)} %negate_multiply_fusion.1, f32[128]{0:T(128)S(1)} %copy-done.73, f32[128]{0:T(128)S(1)} %copy-done.65, f32[8192]{0:T(1024)S(1)} %copy-done.48, f32[8192]{0:T(1024)S(1)} %copy-done.27), kind=kOutput, calls=%fused_computation.182 | convolution fusion | flops 1619001344 | bytes 8553472 | tf_op jit(solution)/shard_map/transpose(jvp())/dot_general | solution.py:17
  714.7 8.2 fusion.217
  722.9 3.7 add_convert_fusion
  726.7 54.1 %while.52 = (s32[]{:T(128)}, f32[768,128]{1,0:T(8,128)}, s32[8,1024]{1,0:T(8,128)}, s32[]{:T(128)}, s32[8,1024]{1,0:T(8,128)}, /*index=5*/bf16[8,1024,128]{2,1,0:T(8,128)(2,1)S(1)}, s32[]{:T(128)}, s32[]{:T(128)}) while((s32[]{:T(128)}, f32[768,128]{1,0:T(8,128)}, s32[8,1024]{1,0:T(8,128)}, s32[]{:T(128)}, ...), condition=%wide.region_34.35_spmd.clone, body=%wide.region_33.34_spmd.clone.sunk | while | flops 215707648 | bytes 1099883 | solution.py:227
  727.6 5.1 fusion.265
  733.5 6.1 fusion.265
  740.4 6.1 fusion.265
  747.3 6.1 fusion.265
  754.1 6.1 fusion.265
  761.0 6.1 fusion.265
  767.9 6.1 fusion.265
  774.8 6.1 fusion.265
  783.9 4.5 all-reduce.21
  789.8 2.5 multiply_reduce_fusion.28
  808.3 3.8 reduce-scatter.3.cloned.1.call-done
  816.6 4.6 concatenate.19
  821.1 40.4 %all-reduce.20 = (f32[4]{0:T(128)S(1)}, f32[4]{0:T(128)S(1)}) all-reduce(f32[4]{0:T(128)S(1)} %pad_maximum_fusion.3, f32[4]{0:T(128)S(1)} %pad_maximum_fusion.4), channel_id=1, replica_groups=mesh['dp'=2,'region'=16] {'dp','region'}, use_global_device_ids=true, to_apply=%region_23.24 | all-reduce | flops 8 | bytes 64 | tf_op jit(solution)/shard_map/psum | solution.py:248
  (373 shorter events, 107.7 us)
Async XLA Ops:
  7.2 230.4 %all-reduce.26.cloned.1.call-start = ((), (), s32[]{:S(2)}) async-start(), calls=%async_computation.2 | async-start | bytes 8388608 | tf_op jit(solution)/shard_map/psum | solution.py:151
  66.6 5.3 copy-start.43
  66.6 5.5 copy-start.15
  66.6 171.0 %copy-start.23 = (s32[8192]{0:T(1024)S(1)}, s32[8192]{0:T(1024)}, u32[]{:S(2)}) copy-start(s32[8192]{0:T(1024)} %param.30) | copy-start | bytes 98308
  66.6 429.4 %reduce-scatter.5.cloned.1.call-start = ((), (), s32[]{:S(2)}) async-start(), calls=%async_computation.5 | async-start | bytes 589824 | tf_op jit(solution)/shard_map/reduce_scatter | solution.py:235
  72.1 174.1 %copy-start.64 = (f32[128]{0:T(128)}, f32[128]{0:T(128)S(1)}, u32[]{:S(2)}) copy-start(f32[128]{0:T(128)S(1)} %get-tuple-element.727) | copy-start | bytes 1540
  72.1 174.1 %copy-start.72 = (f32[128]{0:T(128)}, f32[128]{0:T(128)S(1)}, u32[]{:S(2)}) copy-start(f32[128]{0:T(128)S(1)} %get-tuple-element.726) | copy-start | bytes 1540
  72.2 192.6 %copy-start.66 = (f32[128]{0:T(128)}, f32[128]{0:T(128)S(1)}, u32[]{:S(2)}) copy-start(f32[128]{0:T(128)S(1)} %get-tuple-element.725) | copy-start | bytes 1540
  72.2 192.6 %copy-start.76 = (f32[128]{0:T(128)}, f32[128]{0:T(128)S(1)}, u32[]{:S(2)}) copy-start(f32[128]{0:T(128)S(1)} %get-tuple-element.724) | copy-start | bytes 1540
  72.2 211.5 %copy-start.68 = (f32[128]{0:T(128)}, f32[128]{0:T(128)S(1)}, u32[]{:S(2)}) copy-start(f32[128]{0:T(128)S(1)} %get-tuple-element.723) | copy-start | bytes 1540
  72.2 211.5 %copy-start.74 = (f32[128]{0:T(128)}, f32[128]{0:T(128)S(1)}, u32[]{:S(2)}) copy-start(f32[128]{0:T(128)S(1)} %get-tuple-element.722) | copy-start | bytes 1540
  72.2 218.8 %copy-start.60 = (f32[128]{0:T(128)}, f32[128]{0:T(128)S(1)}, u32[]{:S(2)}) copy-start(f32[128]{0:T(128)S(1)} %get-tuple-element.720) | copy-start | bytes 1540
  72.2 218.8 %copy-start.62 = (f32[128]{0:T(128)}, f32[128]{0:T(128)S(1)}, u32[]{:S(2)}) copy-start(f32[128]{0:T(128)S(1)} %get-tuple-element.721) | copy-start | bytes 1540
  243.7 10.7 %copy-start.4 = (f32[8192,128]{1,0:T(8,128)}, f32[8192,128]{1,0:T(8,128)S(1)}, u32[]{:S(2)}) copy-start(f32[8192,128]{1,0:T(8,128)S(1)} %get-tuple-element.738) | copy-start | bytes 12582916
  243.8 10.7 %copy-start.26 = (f32[8192]{0:T(1024)}, f32[8192]{0:T(1024)S(1)}, u32[]{:S(2)}) copy-start(f32[8192]{0:T(1024)S(1)} %broadcast_multiply_fusion.3) | copy-start | bytes 98308
  246.2 8.3 copy-start.32
  246.2 8.2 copy-start.47
  260.0 9.8 %copy-start.28 = (f32[8192]{0:T(1024)}, f32[8192]{0:T(1024)S(1)}, u32[]{:S(2)}) copy-start(f32[8192]{0:T(1024)S(1)} %broadcast_multiply_fusion.2) | copy-start | bytes 98308
  281.2 7.3 copy-start.6
  281.2 7.3 copy-start.30
  288.6 8.4 copy-start
  291.0 8.3 copy-start.38
  445.4 6.9 copy-start.82
  445.4 50.6 %copy-start.46 = (f32[768]{0:T(1024)S(1)}, f32[768]{0:T(1024)}, u32[]{:S(2)}) copy-start(f32[768]{0:T(1024)} %get-tuple-element.500) | copy-start | bytes 9220
  445.4 50.7 %copy-start.12 = (f32[64,768]{1,0:T(8,128)S(1)}, f32[64,768]{1,0:T(8,128)}, u32[]{:S(2)}) copy-start(f32[64,768]{1,0:T(8,128)} %param.36) | copy-start | bytes 589828
  445.4 50.7 %copy-start.40 = (f32[64,768]{1,0:T(8,128)S(1)}, f32[64,768]{1,0:T(8,128)}, u32[]{:S(2)}) copy-start(f32[64,768]{1,0:T(8,128)} %param.38) | copy-start | bytes 589828
  445.4 50.7 %copy-start.41 = (f32[64,768]{1,0:T(8,128)S(1)}, f32[64,768]{1,0:T(8,128)}, u32[]{:S(2)}) copy-start(f32[64,768]{1,0:T(8,128)} %param.37) | copy-start | bytes 589828
  445.4 183.5 %copy-start.25 = (f32[8192]{0:T(1024)S(1)}, f32[8192]{0:T(1024)}, u32[]{:S(2)}) copy-start(f32[8192]{0:T(1024)} %copy-done.24) | copy-start | bytes 98308
  445.4 183.5 %copy-start.61 = (f32[128]{0:T(128)S(1)}, f32[128]{0:T(128)}, u32[]{:S(2)}) copy-start(f32[128]{0:T(128)} %copy-done.60) | copy-start | bytes 1540
  445.4 183.5 %copy-start.63 = (f32[128]{0:T(128)S(1)}, f32[128]{0:T(128)}, u32[]{:S(2)}) copy-start(f32[128]{0:T(128)} %copy-done.62) | copy-start | bytes 1540
  446.1 182.8 %all-reduce.28.cloned.1.call-start = ((), (), s32[]{:S(2)}) async-start(), calls=%async_computation.3 | async-start | bytes 8388608 | tf_op jit(solution)/shard_map/psum | solution.py:203
  446.9 354.0 %all-reduce.30.cloned.1.call-start = ((), (), s32[]{:S(2)}) async-start(), calls=%async_computation.6 | async-start | bytes 303104 | tf_op jit(solution)/shard_map/psum | solution.py:210
  498.5 138.0 %copy-start.39 = (f32[8192]{0:T(1024)S(1)}, f32[8192]{0:T(1024)}, u32[]{:S(2)}) copy-start(f32[8192]{0:T(1024)} %copy-done.38) | copy-start | bytes 98308
  628.9 7.6 copy-start.1
  628.9 7.6 copy-start.8
  636.6 5.2 copy-start.7
  636.6 5.2 copy-start.31
  636.6 5.2 copy-start.52
  636.6 5.2 copy-start.69
  636.6 5.2 copy-start.75
  641.8 6.4 copy-start.37
  685.2 5.2 copy-start.35
  703.7 11.0 %copy-start.33 = (f32[8192]{0:T(1024)S(1)}, f32[8192]{0:T(1024)}, u32[]{:S(2)}) copy-start(f32[8192]{0:T(1024)} %copy-done.32) | copy-start | bytes 98308
  726.6 54.2 %copy-start.59 = (f32[8,128]{1,0:T(8,128)S(1)}, f32[8,128]{1,0:T(8,128)}, u32[]{:S(2)}) copy-start(f32[8,128]{1,0:T(8,128)} %fusion.117) | copy-start | bytes 12292
  726.6 54.3 %copy-start.70 = (f32[128]{0:T(128)S(1)}, f32[128]{0:T(128)}, u32[]{:S(2)}) copy-start(f32[128]{0:T(128)} %get-tuple-element.582) | copy-start | bytes 1540
  726.6 54.3 %copy-start.71 = (f32[128]{0:T(128)S(1)}, f32[128]{0:T(128)}, u32[]{:S(2)}) copy-start(f32[128]{0:T(128)} %get-tuple-element.583) | copy-start | bytes 1540
  726.7 54.3 %copy-start.78 = (f32[128]{0:T(128)S(1)}, f32[128]{0:T(128)}, u32[]{:S(2)}) copy-start(f32[128]{0:T(128)} %get-tuple-element.585) | copy-start | bytes 1540
  726.7 54.2 %copy-start.79 = (f32[128]{0:T(128)S(1)}, f32[128]{0:T(128)}, u32[]{:S(2)}) copy-start(f32[128]{0:T(128)} %get-tuple-element.591) | copy-start | bytes 1540
  726.7 54.2 %copy-start.80 = (f32[128]{0:T(128)S(1)}, f32[128]{0:T(128)}, u32[]{:S(2)}) copy-start(f32[128]{0:T(128)} %get-tuple-element.587) | copy-start | bytes 1540
  726.7 54.2 %copy-start.81 = (f32[128]{0:T(128)S(1)}, f32[128]{0:T(128)}, u32[]{:S(2)}) copy-start(f32[128]{0:T(128)} %get-tuple-element.592) | copy-start | bytes 1540
  726.7 54.3 %copy-start.55 = (f32[128,128]{1,0:T(8,128)S(1)}, f32[128,128]{1,0:T(8,128)}, u32[]{:S(2)}) copy-start(f32[128,128]{1,0:T(8,128)} %fusion.109) | copy-start | bytes 196612
  726.7 61.6 %copy-start.45 = (f32[129,20]{0,1:T(8,128)S(1)}, f32[129,20]{0,1:T(8,128)}, u32[]{:S(2)}) copy-start(f32[129,20]{0,1:T(8,128)} %param.45) | copy-start | bytes 30964
  726.7 63.0 %copy-start.58 = (f32[1,768]{1,0:T(1,128)S(1)}, f32[1,768]{1,0:T(1,128)}, u32[]{:S(2)}) copy-start(f32[1,768]{1,0:T(1,128)} %param.39) | copy-start | bytes 9220
  780.8 20.1 %copy-start.17 = (f32[290,128]{1,0:T(8,128)S(1)}, f32[290,128]{1,0:T(8,128)}, u32[]{:S(2)}) copy-start(f32[290,128]{1,0:T(8,128)} %param.42) | copy-start | bytes 445444
  780.8 31.3 %copy-start.14 = (f32[768,64]{0,1:T(8,128)S(1)}, f32[768,64]{0,1:T(8,128)}, u32[]{:S(2)}) copy-start(f32[768,64]{0,1:T(8,128)} %param.33) | copy-start | bytes 589828
  780.8 31.3 %copy-start.42 = (f32[768,64]{0,1:T(8,128)S(1)}, f32[768,64]{0,1:T(8,128)}, u32[]{:S(2)}) copy-start(f32[768,64]{0,1:T(8,128)} %param.35) | copy-start | bytes 589828
  780.8 88.5 %copy-start.13 = (f32[64,768]{1,0:T(8,128)S(1)}, f32[64,768]{1,0:T(8,128)}, u32[]{:S(2)}) copy-start(f32[64,768]{1,0:T(8,128)} %param.36) | copy-start | bytes 589828
  780.8 88.5 %copy-start.18 = (f32[64,768]{1,0:T(8,128)S(1)}, f32[64,768]{1,0:T(8,128)}, u32[]{:S(2)}) copy-start(f32[64,768]{1,0:T(8,128)} %get-tuple-element.693) | copy-start | bytes 589828
  780.9 88.5 %copy-start.19 = (f32[64,768]{1,0:T(8,128)S(1)}, f32[64,768]{1,0:T(8,128)}, u32[]{:S(2)}) copy-start(f32[64,768]{1,0:T(8,128)} %get-tuple-element.694) | copy-start | bytes 589828
  783.8 28.3 %reduce-scatter.3.cloned.1.call-start = ((), (), s32[]{:S(2)}) async-start(), calls=%async_computation.4 | async-start | bytes 589824 | tf_op jit(solution)/shard_map/reduce_scatter | solution.py:234
  789.8 81.2 %copy-start.53 = (f32[129,20]{0,1:T(8,128)}, f32[129,20]{0,1:T(8,128)S(1)}, u32[]{:S(2)}) copy-start(f32[129,20]{0,1:T(8,128)S(1)} %get-tuple-element.674) | copy-start | bytes 30964
  789.8 81.2 %copy-start.54 = (f32[129,20]{0,1:T(8,128)}, f32[129,20]{0,1:T(8,128)S(1)}, u32[]{:S(2)}) copy-start(f32[129,20]{0,1:T(8,128)S(1)} %get-tuple-element.675) | copy-start | bytes 30964
  813.9 57.1 %copy-start.20 = (f32[768,64]{0,1:T(8,128)}, f32[768,64]{0,1:T(8,128)S(1)}, u32[]{:S(2)}) copy-start(f32[768,64]{0,1:T(8,128)S(1)} %get-tuple-element.687) | copy-start | bytes 589828
  813.9 57.1 %copy-start.21 = (f32[768,64]{0,1:T(8,128)}, f32[768,64]{0,1:T(8,128)S(1)}, u32[]{:S(2)}) copy-start(f32[768,64]{0,1:T(8,128)S(1)} %get-tuple-element.688) | copy-start | bytes 589828
  (24 other events, 92.0 us)
Sparse Core Ops, SparseCore 0:
  66.8 170.7 all-reduce.25
  446.3 6.7 reduce-scatter.4
  458.7 170.1 all-reduce.27
  783.9 16.9 all-reduce.29
  803.1 9.0 reduce-scatter.2
where the time goes:
time: 888 us; the launch traced here: 878 us
  waiting for transfers between devices  301 us (34%)
  matrix products  299 us (34%)
  other arithmetic  96.1 us (11%)
  blocking collectives  93.8 us (11%)
  local copies, waits for them, and re-layouts  50 us (6%)
  between operations  31.2 us (4%)
    psum x1, waiting for transfers between devices, on_device(): enc_total = lax.psum(partial_pre, 'region')  165 us
    psum x1, waiting for transfers between devices, on_device(): hidden_grad, recon_region = lax.psum((back_hidden, recon_sum), 'region')  130 us
    dot_general x15, matrix products, matmul(): jnp.dot(left, right, precision=highest, preferred_element_type=jnp.float32)  97.3 us
    dot_general x8, matrix products, decode_block(): jnp.dot(hidden_low, dec_low, preferred_element_type=jnp.float32)  87 us
    dot_general x8, matrix products, encode_back(): lax.dot_general(mask_rows, inputs[2], (((0,), (0,)), ((), ())), preferred...  47.4 us
    dot_general x8, matrix products, encode_block(): jnp.dot(mask_rows, enc_low, preferred_element_type=jnp.float32)  44.5 us
    psum x1, blocking collectives, on_device(): hidden_grad, recon_region = lax.psum((back_hidden, recon_sum), 'region')  43.1 us
    psum x1, blocking collectives, on_device(): lax.psum((weight_squares(enc_weight, dec_weight, region_vecs, slot_rows),...  40.4 us
  transfers between devices with their start and end apart: 5, of which 4 were waited for; matrix products, arithmetic and copies ran while one was open for 2% of the time, Pallas kernels for 0%

commit v1 on v0

--- a/solution.py
+++ b/solution.py
@@ -11,6 +11,14 @@
 weight_decay = 0.01
 learn_rate = 0.5
 lamb_eps = 1e-12
+
+
+def add_in_pairs(shard, axis):
+    size, summed = (lax.axis_size(axis), shard)
+    for far in [1 << k for k in range(size.bit_length() - 1)]:
+        route = [(i, i ^ far) for i in range(size)]
+        summed = summed + lax.ppermute(summed, axis, route)
+    return summed
 
 
 def matmul(left, right):
@@ -148,7 +156,7 @@
         jnp.float32
     )
     onehot_low = onehot.astype(jnp.bfloat16)
-    enc_total = lax.psum(partial_pre, "region")
+    enc_total = add_in_pairs(partial_pre, "region")
     pre_one = enc_total + matmul(onehot, trunk_rows[:BATCHES])
     (decoded, diverge), pull_back = jax.vjp(
         lambda pre_in, weights, head_part: trunk_forward(

time: 888 us -> 1170 us (1.32)
  waiting for transfers between devices: 301 us -> 568 us
    ppermute x0 -> x4, waiting for transfers between devices: none -> 441 us  [add_in_pairs(): summed = summed + lax.ppermute(summed, axis, route)]
    psum x1 -> x0, waiting for transfers between devices: 165 us -> none  [on_device(): enc_total = lax.psum(partial_pre, 'region')]
    reduce_sum x4 -> x5, other arithmetic: 23.7 us -> 28.7 us  [layer_norm(): centre = values - jnp.mean(values, axis=-1, keepdims=True)]
  transfers between devices with their start and end apart: 5 -> 8, of which waited for: 4 -> 7; matrix products, arithmetic and copies ran while one was open for 2% -> 2% of each run, Pallas kernels for 0% -> 0%
where the time goes in v1:
time: 1170 us; the launch traced here: 1160 us
  waiting for transfers between devices  568 us (49%)
  matrix products  297 us (25%)
  other arithmetic  107 us (9%)
  blocking collectives  96.1 us (8%)
  local copies, waits for them, and re-layouts  49.2 us (4%)
  between operations  32.6 us (3%)
    ppermute x4, waiting for transfers between devices, add_in_pairs(): summed = summed + lax.ppermute(summed, axis, route)  441 us
    psum x1, waiting for transfers between devices, on_device(): hidden_grad, recon_region = lax.psum((back_hidden, recon_sum), 'region')  120 us
    dot_general x15, matrix products, matmul(): jnp.dot(left, right, precision=highest, preferred_element_type=jnp.float32)  94.6 us
    dot_general x8, matrix products, decode_block(): jnp.dot(hidden_low, dec_low, preferred_element_type=jnp.float32)  87 us
    dot_general x8, matrix products, encode_back(): lax.dot_general(mask_rows, inputs[2], (((0,), (0,)), ((), ())), preferred...  47.4 us
    psum x1, blocking collectives, on_device(): hidden_grad, recon_region = lax.psum((back_hidden, recon_sum), 'region')  45.1 us
    dot_general x8, matrix products, encode_block(): jnp.dot(mask_rows, enc_low, preferred_element_type=jnp.float32)  44.5 us
    psum x1, blocking collectives, on_device(): lax.psum((weight_squares(enc_weight, dec_weight, region_vecs, slot_rows),...  40.5 us
  transfers between devices with their start and end apart: 8, of which 7 were waited for; matrix products, arithmetic and copies ran while one was open for 2% of the time, Pallas kernels for 0%

profile of v1, /device:TPU:0, one launch (start us, length us, event | category | flops | bytes accessed | tf_op | source)
XLA Modules:
  0.0 1163.4 jit_solution(13957853852231010259)
XLA Ops:
  16.3 51.1 %while.50 = (s32[]{:T(128)}, f32[8,1024,128]{2,1,0:T(8,128)}, s32[8,1024]{1,0:T(8,128)}, s32[]{:T(128)}, s32[8,1024]{1,0:T(8,128)}, /*index=5*/bf16[768,128]{1,0:T(8,128)(2,1)S(1)}, s32[]{:T(128)}) while((s32[]{:T(128)}, f32[8,1024,128]{2,1,0:T(8,128)}, s32[8,1024]{1,0:T(8,128)}, s32[]{:T(128)}, s32[8,1024]{1,0:T(8,128)}, ...), condition=%wide.region_1.2_spmd, body=%wide.region_0.1_spmd.sunk | while | flops 215511040 | bytes 770645 | solution.py:151
  17.1 5.6 fusion.255
  23.5 5.6 fusion.255
  29.9 5.6 fusion.255
  36.2 5.6 fusion.255
  42.6 5.6 fusion.255
  49.0 5.6 fusion.255
  55.4 5.6 fusion.255
  61.8 5.6 fusion.255
  67.4 2.8 collective-permute-start
  70.2 91.1 %collective-permute-done = f32[8192,128]{1,0:T(8,128)S(1)} collective-permute-done((f32[8192,128]{1,0:T(8,128)}, f32[8192,128]{1,0:T(8,128)S(1)}, u32[]{:S(2)}, u32[]{:S(2)}) %collective-permute-start) | collective-permute-done | bytes 4194336 | tf_op jit(solution)/shard_map/ppermute | solution.py:20
  161.3 2.7 bitcast_add_fusion
  165.9 90.3 %collective-permute-done.1 = f32[8192,128]{1,0:T(8,128)S(1)} collective-permute-done((f32[8192,128]{1,0:T(8,128)S(1)}, f32[8192,128]{1,0:T(8,128)S(1)}, u32[]{:S(2)}, u32[]{:S(2)}) %collective-permute-start.1) | collective-permute-done | bytes 4194336 | tf_op jit(solution)/shard_map/ppermute | solution.py:20
  258.3 89.7 %collective-permute-done.2 = f32[8192,128]{1,0:T(8,128)S(1)} collective-permute-done((f32[8192,128]{1,0:T(8,128)S(1)}, f32[8192,128]{1,0:T(8,128)S(1)}, u32[]{:S(2)}, u32[]{:S(2)}) %collective-permute-start.2) | collective-permute-done | bytes 4194336 | tf_op jit(solution)/shard_map/ppermute | solution.py:20
  358.1 3.4 fusion.167
  361.6 170.2 %collective-permute-done.3 = f32[8192,128]{1,0:T(8,128)} collective-permute-done((f32[8192,128]{1,0:T(8,128)}, f32[8192,128]{1,0:T(8,128)}, u32[]{:S(2)}, u32[]{:S(2)}) %collective-permute-start.3) | collective-permute-done | bytes 4194336 | tf_op jit(solution)/shard_map/ppermute | solution.py:20
  531.7 4.9 fusion.224
  539.2 8.2 fusion.227
  547.4 5.6 copy.58
  553.0 4.7 multiply_reduce_fusion.10
  557.8 5.1 convolution_add_fusion.2
  562.9 6.7 fusion.189
  569.6 4.6 fusion.228
  576.7 4.9 fusion.229
  584.6 5.3 fusion.102
  592.3 146.1 %while.51 = (s32[]{:T(128)}, f32[128,768]{1,0:T(8,128)S(1)}, f32[768]{0:T(1024)S(1)}, f32[768]{0:T(1024)}, f32[]{:T(128)}, /*index=5*/f32[8,1024,128]{2,1,0:T(8,...) while((s32[]{:T(128)}, f32[128,768]{1,0:T(8,128)S(1)}, ...), condition=%wide.region_14.15_spmd.clone, body=%wide.region_10.14_spmd.clone.sunk | while | flops 643528960 | bytes 19630788 | solution.py:207
  594.1 10.9 fusion.262
  612.3 10.9 fusion.262
  630.5 10.9 fusion.262
  648.8 10.9 fusion.262
  667.0 10.9 fusion.262
  685.3 10.9 fusion.262
  703.5 10.9 fusion.262
  721.7 10.9 fusion.262
  745.8 45.1 %psum.56 = f32[]{:T(128)} all-reduce(f32[]{:T(128)} %get-tuple-element.495), channel_id=1, replica_groups=mesh['dp'=2,'region'=16] {'region'}, use_global_device_ids=true, to_apply=%region_15.16 | all-reduce | flops 1 | bytes 8 | tf_op jit(solution)/shard_map/psum | solution.py:211
  793.3 120.4 %all-reduce.25.cloned.1.call-done = f32[8192,128]{1,0:T(8,128)} async-done(((f32[8192,128]{1,0:T(8,128)}), f32[8192,128]{1,0:T(8,128)}) %all-reduce.25.cloned.1.call-update) | async-done | bytes 4194320 | tf_op jit(solution)/shard_map/psum | solution.py:211
  913.8 7.6 fusion.210
  921.5 5.1 fusion.223
  926.7 6.4 multiply_reduce_fusion.2
  933.1 5.3 fusion.222
  938.4 4.5 multiply_add_fusion.9
  943.2 4.4 fusion.122
  947.6 11.2 multiply_reduce_fusion.1
  958.8 11.3 fusion.109
  972.5 2.7 fusion.115
  975.3 5.1 fusion.220
  980.5 8.0 multiply_reduce_fusion
  988.5 10.9 fusion.103
  999.5 8.2 fusion.219
  1007.8 3.7 add_convert_fusion
  1011.6 54.1 %while.52 = (s32[]{:T(128)}, f32[768,128]{1,0:T(8,128)}, s32[8,1024]{1,0:T(8,128)}, s32[]{:T(128)}, s32[8,1024]{1,0:T(8,128)}, /*index=5*/bf16[8,1024,128]{2,1,0:T(8,128)(2,1)S(1)}, s32[]{:T(128)}, s32[]{:T(128)}) while((s32[]{:T(128)}, f32[768,128]{1,0:T(8,128)}, s32[8,1024]{1,0:T(8,128)}, s32[]{:T(128)}, ...), condition=%wide.region_33.34_spmd.clone, body=%wide.region_32.33_spmd.clone.sunk | while | flops 215707648 | bytes 1099883 | solution.py:235
  1012.5 5.1 fusion.267
  1018.3 6.1 fusion.267
  1025.2 6.1 fusion.267
  1032.1 6.1 fusion.267
  1039.0 6.1 fusion.267
  1045.8 6.1 fusion.267
  1052.7 6.1 fusion.267
  1059.6 6.1 fusion.267
  1068.7 4.5 all-reduce.21
  1074.6 2.5 multiply_reduce_fusion.28
  1093.2 3.9 reduce-scatter.3.cloned.1.call-done
  1101.5 4.6 concatenate.19
  1106.1 40.5 %all-reduce.20 = (f32[4]{0:T(128)S(1)}, f32[4]{0:T(128)S(1)}) all-reduce(f32[4]{0:T(128)S(1)} %pad_maximum_fusion.3, f32[4]{0:T(128)S(1)} %pad_maximum_fusion.4), channel_id=1, replica_groups=mesh['dp'=2,'region'=16] {'dp','region'}, use_global_device_ids=true, to_apply=%region_22.23 | all-reduce | flops 8 | bytes 64 | tf_op jit(solution)/shard_map/psum | solution.py:256
  (382 shorter events, 129.7 us)
Async XLA Ops:
  8.0 782.9 %reduce-scatter.5.cloned.1.call-start = ((), (), s32[]{:S(2)}) async-start(), calls=%async_computation.4 | async-start | bytes 589824 | tf_op jit(solution)/shard_map/reduce_scatter | solution.py:243
  67.4 93.9 %collective-permute-start = (f32[8192,128]{1,0:T(8,128)}, f32[8192,128]{1,0:T(8,128)S(1)}, u32[]{:S(2)}, u32[]{:S(2)}) collective-permute-start(f32[8192,128]{1,0:T(8,128)} %bitcast.124), channel_id=1, source_target_pairs={{0,1},{1,0},{2,3},{3,2},{4,5},{5,4},{6,7},{7,6},{8,9},{9,8},{10,11... | collective-permute-start | bytes 12582920 | tf_op jit(solution)/shard_map/ppermute | solution.py:20
  164.0 92.2 %collective-permute-start.1 = (f32[8192,128]{1,0:T(8,128)S(1)}, f32[8192,128]{1,0:T(8,128)S(1)}, u32[]{:S(2)}, u32[]{:S(2)}) collective-permute-start(f32[8192,128]{1,0:T(8,128)S(1)} %bitcast_add_fusion), channel_id=1, source_target_pairs={{0,2},{1,3},{2,0},{3,1},{4,6},{5,7},{6,4},{7,5},{8,10},{9,11},{10,... | collective-permute-start | bytes 12582920 | tf_op jit(solution)/shard_map/ppermute | solution.py:20
  256.6 95.9 %copy-start.11 = (f32[64,768]{1,0:T(8,128)S(1)}, f32[64,768]{1,0:T(8,128)}, u32[]{:S(2)}) copy-start(f32[64,768]{1,0:T(8,128)} %param.36) | copy-start | bytes 589828
  256.7 95.9 %copy-start.56 = (f32[8192]{0:T(1024)S(1)}, f32[8192]{0:T(1024)}, u32[]{:S(2)}) copy-start(f32[8192]{0:T(1024)} %param.32) | copy-start | bytes 98308
  256.7 96.5 %copy-start.57 = (f32[1,768]{1,0:T(1,128)S(1)}, f32[1,768]{1,0:T(1,128)}, u32[]{:S(2)}) copy-start(f32[1,768]{1,0:T(1,128)} %param.39) | copy-start | bytes 9220
  256.7 100.5 %copy-start.43 = (f32[129,20]{0,1:T(8,128)S(1)}, f32[129,20]{0,1:T(8,128)}, u32[]{:S(2)}) copy-start(f32[129,20]{0,1:T(8,128)} %param.45) | copy-start | bytes 30964
  256.7 100.7 %copy-start.15 = (f32[290,128]{1,0:T(8,128)S(1)}, f32[290,128]{1,0:T(8,128)}, u32[]{:S(2)}) copy-start(f32[290,128]{1,0:T(8,128)} %param.42) | copy-start | bytes 445444
  256.7 101.4 %copy-start.23 = (s32[8192]{0:T(1024)S(1)}, s32[8192]{0:T(1024)}, u32[]{:S(2)}) copy-start(s32[8192]{0:T(1024)} %param.30) | copy-start | bytes 98308
  256.7 91.3 %collective-permute-start.2 = (f32[8192,128]{1,0:T(8,128)S(1)}, f32[8192,128]{1,0:T(8,128)S(1)}, u32[]{:S(2)}, u32[]{:S(2)}) collective-permute-start(f32[8192,128]{1,0:T(8,128)S(1)} %add.711), channel_id=1, source_target_pairs={{0,4},{1,5},{2,6},{3,7},{4,0},{5,1},{6,2},{7,3},{8,12},{9,13},{10,... | collective-permute-start | bytes 12582920 | tf_op jit(solution)/shard_map/ppermute | solution.py:20
  350.4 181.4 %collective-permute-start.3 = (f32[8192,128]{1,0:T(8,128)}, f32[8192,128]{1,0:T(8,128)}, u32[]{:S(2)}, u32[]{:S(2)}) collective-permute-start(f32[8192,128]{1,0:T(8,128)} %add.712), channel_id=1, source_target_pairs={{0,8},{1,9},{2,10},{3,11},{4,12},{5,13},{6,14},{7,15},{8,0},{9,1},... | collective-permute-start | bytes 12582920 | tf_op jit(solution)/shard_map/ppermute | solution.py:20
  357.4 181.7 %copy-start.64 = (f32[128]{0:T(128)}, f32[128]{0:T(128)S(1)}, u32[]{:S(2)}) copy-start(f32[128]{0:T(128)S(1)} %get-tuple-element.729) | copy-start | bytes 1540
  357.4 181.7 %copy-start.72 = (f32[128]{0:T(128)}, f32[128]{0:T(128)S(1)}, u32[]{:S(2)}) copy-start(f32[128]{0:T(128)S(1)} %get-tuple-element.728) | copy-start | bytes 1540
  357.4 200.3 %copy-start.66 = (f32[128]{0:T(128)}, f32[128]{0:T(128)S(1)}, u32[]{:S(2)}) copy-start(f32[128]{0:T(128)S(1)} %get-tuple-element.727) | copy-start | bytes 1540
  357.4 200.3 %copy-start.76 = (f32[128]{0:T(128)}, f32[128]{0:T(128)S(1)}, u32[]{:S(2)}) copy-start(f32[128]{0:T(128)S(1)} %get-tuple-element.726) | copy-start | bytes 1540
  357.5 219.2 %copy-start.68 = (f32[128]{0:T(128)}, f32[128]{0:T(128)S(1)}, u32[]{:S(2)}) copy-start(f32[128]{0:T(128)S(1)} %get-tuple-element.725) | copy-start | bytes 1540
  357.5 219.2 %copy-start.74 = (f32[128]{0:T(128)}, f32[128]{0:T(128)S(1)}, u32[]{:S(2)}) copy-start(f32[128]{0:T(128)S(1)} %get-tuple-element.724) | copy-start | bytes 1540
  357.5 226.5 %copy-start.60 = (f32[128]{0:T(128)}, f32[128]{0:T(128)S(1)}, u32[]{:S(2)}) copy-start(f32[128]{0:T(128)S(1)} %get-tuple-element.722) | copy-start | bytes 1540
  357.5 226.5 %copy-start.62 = (f32[128]{0:T(128)}, f32[128]{0:T(128)S(1)}, u32[]{:S(2)}) copy-start(f32[128]{0:T(128)S(1)} %get-tuple-element.723) | copy-start | bytes 1540
  536.7 10.7 copy-start.4
  536.7 10.7 copy-start.26
  539.1 8.3 copy-start.32
  539.1 8.2 copy-start.47
  553.0 9.9 copy-start.28
  574.2 7.3 copy-start.6
  574.2 7.3 copy-start.30
  581.6 8.4 copy-start
  584.0 8.3 copy-start.38
  738.4 6.7 copy-start.82
  738.4 52.5 %copy-start.46 = (f32[768]{0:T(1024)S(1)}, f32[768]{0:T(1024)}, u32[]{:S(2)}) copy-start(f32[768]{0:T(1024)} %get-tuple-element.500) | copy-start | bytes 9220
  738.4 52.5 %copy-start.12 = (f32[64,768]{1,0:T(8,128)S(1)}, f32[64,768]{1,0:T(8,128)}, u32[]{:S(2)}) copy-start(f32[64,768]{1,0:T(8,128)} %param.36) | copy-start | bytes 589828
  738.4 52.5 %copy-start.40 = (f32[64,768]{1,0:T(8,128)S(1)}, f32[64,768]{1,0:T(8,128)}, u32[]{:S(2)}) copy-start(f32[64,768]{1,0:T(8,128)} %param.38) | copy-start | bytes 589828
  738.4 52.5 %copy-start.41 = (f32[64,768]{1,0:T(8,128)S(1)}, f32[64,768]{1,0:T(8,128)}, u32[]{:S(2)}) copy-start(f32[64,768]{1,0:T(8,128)} %param.37) | copy-start | bytes 589828
  738.4 175.3 %copy-start.25 = (f32[8192]{0:T(1024)S(1)}, f32[8192]{0:T(1024)}, u32[]{:S(2)}) copy-start(f32[8192]{0:T(1024)} %copy-done.24) | copy-start | bytes 98308
  738.4 175.3 %copy-start.61 = (f32[128]{0:T(128)S(1)}, f32[128]{0:T(128)}, u32[]{:S(2)}) copy-start(f32[128]{0:T(128)} %copy-done.60) | copy-start | bytes 1540
  738.5 175.3 %copy-start.63 = (f32[128]{0:T(128)S(1)}, f32[128]{0:T(128)}, u32[]{:S(2)}) copy-start(f32[128]{0:T(128)} %copy-done.62) | copy-start | bytes 1540
  739.1 174.6 %all-reduce.25.cloned.1.call-start = ((), (), s32[]{:S(2)}) async-start(), calls=%async_computation.2 | async-start | bytes 8388608 | tf_op jit(solution)/shard_map/psum | solution.py:211
  739.7 346.1 %all-reduce.27.cloned.1.call-start = ((), (), s32[]{:S(2)}) async-start(), calls=%async_computation.5 | async-start | bytes 303104 | tf_op jit(solution)/shard_map/psum | solution.py:218
  793.3 128.0 %copy-start.39 = (f32[8192]{0:T(1024)S(1)}, f32[8192]{0:T(1024)}, u32[]{:S(2)}) copy-start(f32[8192]{0:T(1024)} %copy-done.38) | copy-start | bytes 98308
  913.8 7.6 copy-start.1
  913.8 7.6 copy-start.8
  926.7 6.4 copy-start.37
  988.5 11.0 copy-start.33
  1011.5 54.2 %copy-start.59 = (f32[8,128]{1,0:T(8,128)S(1)}, f32[8,128]{1,0:T(8,128)}, u32[]{:S(2)}) copy-start(f32[8,128]{1,0:T(8,128)} %fusion.117) | copy-start | bytes 12292
  1011.5 54.3 %copy-start.70 = (f32[128]{0:T(128)S(1)}, f32[128]{0:T(128)}, u32[]{:S(2)}) copy-start(f32[128]{0:T(128)} %get-tuple-element.582) | copy-start | bytes 1540
  1011.5 54.3 %copy-start.71 = (f32[128]{0:T(128)S(1)}, f32[128]{0:T(128)}, u32[]{:S(2)}) copy-start(f32[128]{0:T(128)} %get-tuple-element.583) | copy-start | bytes 1540
  1011.5 54.3 %copy-start.78 = (f32[128]{0:T(128)S(1)}, f32[128]{0:T(128)}, u32[]{:S(2)}) copy-start(f32[128]{0:T(128)} %get-tuple-element.585) | copy-start | bytes 1540
  1011.5 54.2 %copy-start.79 = (f32[128]{0:T(128)S(1)}, f32[128]{0:T(128)}, u32[]{:S(2)}) copy-start(f32[128]{0:T(128)} %get-tuple-element.591) | copy-start | bytes 1540
  1011.5 54.2 %copy-start.80 = (f32[128]{0:T(128)S(1)}, f32[128]{0:T(128)}, u32[]{:S(2)}) copy-start(f32[128]{0:T(128)} %get-tuple-element.587) | copy-start | bytes 1540
  1011.5 54.2 %copy-start.81 = (f32[128]{0:T(128)S(1)}, f32[128]{0:T(128)}, u32[]{:S(2)}) copy-start(f32[128]{0:T(128)} %get-tuple-element.592) | copy-start | bytes 1540
  1011.5 54.3 %copy-start.55 = (f32[128,128]{1,0:T(8,128)S(1)}, f32[128,128]{1,0:T(8,128)}, u32[]{:S(2)}) copy-start(f32[128,128]{1,0:T(8,128)} %fusion.109) | copy-start | bytes 196612
  1011.6 61.6 %copy-start.45 = (f32[129,20]{0,1:T(8,128)S(1)}, f32[129,20]{0,1:T(8,128)}, u32[]{:S(2)}) copy-start(f32[129,20]{0,1:T(8,128)} %param.45) | copy-start | bytes 30964
  1011.6 63.0 %copy-start.58 = (f32[1,768]{1,0:T(1,128)S(1)}, f32[1,768]{1,0:T(1,128)}, u32[]{:S(2)}) copy-start(f32[1,768]{1,0:T(1,128)} %param.39) | copy-start | bytes 9220
  1065.7 20.1 %copy-start.17 = (f32[290,128]{1,0:T(8,128)S(1)}, f32[290,128]{1,0:T(8,128)}, u32[]{:S(2)}) copy-start(f32[290,128]{1,0:T(8,128)} %param.42) | copy-start | bytes 445444
  1065.7 31.4 %copy-start.14 = (f32[768,64]{0,1:T(8,128)S(1)}, f32[768,64]{0,1:T(8,128)}, u32[]{:S(2)}) copy-start(f32[768,64]{0,1:T(8,128)} %param.33) | copy-start | bytes 589828
  1065.7 31.4 %copy-start.42 = (f32[768,64]{0,1:T(8,128)S(1)}, f32[768,64]{0,1:T(8,128)}, u32[]{:S(2)}) copy-start(f32[768,64]{0,1:T(8,128)} %param.35) | copy-start | bytes 589828
  1065.7 88.7 %copy-start.13 = (f32[64,768]{1,0:T(8,128)S(1)}, f32[64,768]{1,0:T(8,128)}, u32[]{:S(2)}) copy-start(f32[64,768]{1,0:T(8,128)} %param.36) | copy-start | bytes 589828
  1065.7 88.7 %copy-start.18 = (f32[64,768]{1,0:T(8,128)S(1)}, f32[64,768]{1,0:T(8,128)}, u32[]{:S(2)}) copy-start(f32[64,768]{1,0:T(8,128)} %get-tuple-element.693) | copy-start | bytes 589828
  1065.7 88.7 %copy-start.19 = (f32[64,768]{1,0:T(8,128)S(1)}, f32[64,768]{1,0:T(8,128)}, u32[]{:S(2)}) copy-start(f32[64,768]{1,0:T(8,128)} %get-tuple-element.694) | copy-start | bytes 589828
  1068.6 28.4 %reduce-scatter.3.cloned.1.call-start = ((), (), s32[]{:S(2)}) async-start(), calls=%async_computation.3 | async-start | bytes 589824 | tf_op jit(solution)/shard_map/reduce_scatter | solution.py:242
  1074.6 81.4 %copy-start.53 = (f32[129,20]{0,1:T(8,128)}, f32[129,20]{0,1:T(8,128)S(1)}, u32[]{:S(2)}) copy-start(f32[129,20]{0,1:T(8,128)S(1)} %get-tuple-element.674) | copy-start | bytes 30964
  1074.6 81.4 %copy-start.54 = (f32[129,20]{0,1:T(8,128)}, f32[129,20]{0,1:T(8,128)S(1)}, u32[]{:S(2)}) copy-start(f32[129,20]{0,1:T(8,128)S(1)} %get-tuple-element.675) | copy-start | bytes 30964
  1098.9 57.1 %copy-start.20 = (f32[768,64]{0,1:T(8,128)}, f32[768,64]{0,1:T(8,128)S(1)}, u32[]{:S(2)}) copy-start(f32[768,64]{0,1:T(8,128)S(1)} %get-tuple-element.687) | copy-start | bytes 589828
  1098.9 57.1 %copy-start.21 = (f32[768,64]{0,1:T(8,128)}, f32[768,64]{0,1:T(8,128)S(1)}, u32[]{:S(2)}) copy-start(f32[768,64]{0,1:T(8,128)S(1)} %get-tuple-element.688) | copy-start | bytes 589828
  (27 other events, 119.6 us)
Sparse Core Ops, SparseCore 0:
  739.3 8.1 reduce-scatter.4
  1068.8 16.9 all-reduce.26
  1088.0 8.9 reduce-scatter.2
Sparse Core Ops, SparseCore 1:
  745.3 168.4 all-reduce.24
